TPU v7x, 128 devices: a whole 4x4x4 slice. The times are simulated.
128 devices in a mesh: dp: 32 (over x, y, core), tensor: 4 (over z).
Axes of the slice: x: 4, y: 4, z: 4, core: 2. Of those that a mesh axis runs over, the one named last changes fastest.
Arguments:
- inputs: bfloat16 [16384, 1024], P(('dp', 'tensor')), may hold values from -6 to 6
- lengths: int32 [32], replicated, may hold values from 1 to 16, 128 in all
- w_qkv: bfloat16 [1, 1024, 3, 1024], P(None, 'dp', None, 'tensor'), may hold values from -0.1875 to 0.1875
- w_out: bfloat16 [1, 1024, 1024], P(None, 'tensor', 'dp'), may hold values from -0.75 to 0.75
- w_fc: bfloat16 [1, 1024, 4096], P(None, 'dp', 'tensor'), may hold values from -0.1875 to 0.1875
- w_proj: bfloat16 [1, 4096, 1024], P(None, 'tensor', 'dp'), may hold values from -0.09375 to 0.09375
- b_qv: bfloat16 [1, 2, 1024], P(None, None, ('tensor', 'dp')), may hold values from -3 to 3
- b_fc: bfloat16 [1, 4096], P(None, ('tensor', 'dp')), may hold values from -3 to 3
- gains: float32 [1, 2, 1024], P(None, None, ('dp', 'tensor')), may hold values from 0.5 to 1.5
- shifts: float32 [1, 4, 1024], P(None, None, ('dp', 'tensor')), may hold values from -2 to 2
- cotangent: bfloat16 [16384, 1024], P(('dp', 'tensor')), may hold values from -24 to 24
Outputs:
- outputs: float32 [16384, 1024], P(('dp', 'tensor'))
- grad_inputs: float32 [16384, 1024], P(('dp', 'tensor'))
- grad_w_qkv: float32 [1, 1024, 3, 1024], P(None, 'dp', None, 'tensor')
- grad_w_out: float32 [1, 1024, 1024], P(None, 'tensor', 'dp')
- grad_w_fc: float32 [1, 1024, 4096], P(None, 'dp', 'tensor')
- grad_w_proj: float32 [1, 4096, 1024], P(None, 'tensor', 'dp')
- grad_b_qv: float32 [1, 2, 1024], P(None, None, ('tensor', 'dp'))
- grad_b_fc: float32 [1, 4096], P(None, ('tensor', 'dp'))
- grad_gains: float32 [1, 2, 1024], P(None, None, ('dp', 'tensor'))
- grad_shifts: float32 [1, 4, 1024], P(None, None, ('dp', 'tensor'))
Inputs may be any that keep to these rules, and one draw needn't show every extreme that they name: lengths counts blocks of 128 tokens; the lengths sum to 128 and the longest is exactly 16.
All inputs are finite; a program needn't handle non-finite values.
Results may differ from a plain program's by a relative error of at most 0.012.
Values may be sent and summed in bfloat16 or wider, within the bound.
A program may use at most 192 MiB of HBM per device.

v0:
```python
import functools

import jax
import jax.numpy as jnp
from jax import lax
from jax.experimental import pallas as pl
from jax.experimental.pallas import tpu as pltpu
from jax.sharding import PartitionSpec as P

HEAD_DIM = 64
BLOCK = 128
D = 1024
GROUP = 512
SPAN = 512
BF = jnp.bfloat16
F32 = jnp.float32
MESH = pl.DeviceIdType.MESH
VMEM_LIMIT = 58 * 1024 * 1024


def nn(a, b):
    return jnp.dot(a, b, preferred_element_type=F32)


def nt(a, b):
    return lax.dot_general(a, b, (((1,), (1,)), ((), ())), preferred_element_type=F32)


def tn(a, b):
    return lax.dot_general(a, b, (((0,), (0,)), ((), ())), preferred_element_type=F32)


def rows(start, size, step=None):
    return pl.ds(pl.multiple_of(start, step or size), size)


class Place:
    def __init__(self):
        self.dp = lax.axis_index("dp")
        self.z = lax.axis_index("tensor")
        self.c = lax.rem(self.dp, 2)
        self.chip = self.dp // 2
        self.y = lax.rem(self.chip, 4)
        self.x = self.chip // 4

    def at(self, dx=0, dy=0, dz=0, flip=False):
        x = lax.rem(self.x + dx + 4, 4)
        y = lax.rem(self.y + dy + 4, 4)
        c = 1 - self.c if flip else self.c
        return ((x * 4 + y) * 2 + c, lax.rem(self.z + dz + 4, 4))

    def linear(self, step):
        return (lax.rem(self.chip + step + 16, 16) * 2 + self.c, self.z)

    def beside(self, dy, step):
        chip = self.x * 4 + lax.rem(self.y + dy + 4, 4)
        return (lax.rem(chip + step + 16, 16) * 2 + self.c, self.z)

    def beside_source(self, step=2, dy=-1):
        chip = lax.rem(self.chip - step + 16, 16)
        y = lax.rem(lax.rem(chip, 4) + dy + 4, 4)
        return ((chip // 4 * 4 + y) * 2 + self.c, self.z)


class Copies:
    def __init__(self, send_sem, recv_sem):
        self.send_sem, self.recv_sem = send_sem, recv_sem
        self.started, self.settled = [], []

    def put(self, src, dst, device):
        k = len(self.started)
        copy = pltpu.make_async_remote_copy(
            src_ref=src,
            dst_ref=dst,
            send_sem=self.send_sem.at[k],
            recv_sem=self.recv_sem.at[k],
            device_id=device,
            device_id_type=MESH,
        )
        copy.start()
        self.started.append(copy)
        return copy

    def settle(self, *copies):
        for copy in copies:
            copy.wait_send()
            self.settled.append(copy)

    def finish(self):
        for copy in self.started:
            if not any(copy is other for other in self.settled):
                copy.wait_send()


def greet(devices):
    barrier = pltpu.get_barrier_semaphore()
    for device in devices:
        pl.semaphore_signal(barrier, inc=1, device_id=device, device_id_type=MESH)
    pl.semaphore_wait(barrier, len(devices))


class RingGather:
    def __init__(self, copies, place, buf, size=BLOCK):
        self.copies, self.place, self.buf, self.size = copies, place, buf, size

    def block(self, dz, part=None):
        start = lax.rem(self.place.z + dz + 4, 4) * self.size
        if part is None:
            return self.buf.at[rows(start, self.size)]
        half = self.size // 2
        return self.buf.at[rows(start + part * half, half)]

    def start(self):
        own = self.block(0)
        self.up = self.copies.put(own, own, self.place.at(dz=1))
        self.down = self.copies.put(own, own, self.place.at(dz=-1))

    def below(self):
        self.up.wait_recv()
        half = self.block(-1, 0)
        self.up2 = self.copies.put(half, half, self.place.at(dz=1))

    def above(self):
        self.down.wait_recv()
        half = self.block(1, 1)
        self.down2 = self.copies.put(half, half, self.place.at(dz=-1))

    def far(self):
        self.up2.wait_recv()
        self.down2.wait_recv()


class DirectGather:
    copies_needed = 31

    def __init__(self, copies, place, w):
        self.copies, self.place, self.w = copies, place, w
        self.shared = []

    def dev(self, axis, step):
        c = self.place.c
        if axis == 0:
            return self.place.at(dx=c * step, dy=(1 - c) * step)
        return self.place.at(dx=(1 - c) * step, dy=c * step)

    def block(self, a, b):
        p, c = self.place, self.place.c
        x = lax.rem(p.x + b * (1 - c) + a * c + 4, 4)
        y = lax.rem(p.y + a * (1 - c) + b * c + 4, 4)
        return self.w.at[rows(((x * 4 + y) * 2 + c) * 32, 32)]

    def put(self, ref, device):
        return self.copies.put(ref, ref, device)

    def spread(self, a):
        ref = self.block(a, 0)
        self.second[a] = [self.put(ref, self.dev(1, step)) for step in (1, -1, 2)]
        self.shared.append(self.put(ref, self.place.at(flip=True)))

    def start(self):
        ref = self.block(0, 0)
        self.first = [self.put(ref, self.dev(0, step)) for step in (1, -1, 2)]
        self.second = {}
        self.spread(0)

    def step1(self):
        for copy, a in zip(self.first, (-1, 1, 2)):
            copy.wait_recv()
            self.spread(a)

    def step2(self):
        for a in (0, -1, 1, 2):
            for copy, b in zip(self.second[a], (-1, 1, 2)):
                copy.wait_recv()
                self.shared.append(self.put(self.block(a, b), self.place.at(flip=True)))

    def step3(self):
        for copy in self.shared:
            copy.wait_recv()


class PlaneGather:
    def __init__(self, copies, place, w, first, width):
        self.copies, self.place, self.w = copies, place, w
        c = place.c
        self.first, self.width = first, width
        self.cols = pl.ds(pl.multiple_of(first + c * (width // 2), 128), width // 2)

    def dev(self, axis, step):
        if axis == 0:
            return self.place.at(dy=step)
        return self.place.at(dx=step)

    def block(self, first_off, second_off, part=None):
        p = self.place
        start = (lax.rem(p.x + second_off + 4, 4) * 4 + lax.rem(p.y + first_off + 4, 4)) * 64
        if part is None:
            return self.w.at[rows(start, 64), self.cols]
        return self.w.at[rows(start + 32 * part, 32), self.cols]

    def put(self, ref, device):
        return self.copies.put(ref, ref, device)

    def start(self):
        p = self.place
        mine = self.w.at[rows(p.dp * 32, 32), pl.ds(self.first, self.width)]
        self.swap = self.put(mine, p.at(flip=True))

    def spread(self, first_off):
        ref = self.block(first_off, 0)
        return (self.put(ref, self.dev(1, 1)), self.put(ref, self.dev(1, -1)))

    def share(self, first_off, second_off):
        self.shared.append(self.put(self.block(first_off, second_off), self.place.at(flip=True)))

    def step1(self):
        self.swap.wait_recv()
        ref = self.block(0, 0)
        self.shared = []
        self.up = self.put(ref, self.dev(0, 1))
        self.down = self.put(ref, self.dev(0, -1))
        self.out = {0: self.spread(0)}

    def step2(self):
        self.up.wait_recv()
        self.up2 = self.put(self.block(-1, 0, 0), self.dev(0, 1))
        self.down.wait_recv()
        self.down2 = self.put(self.block(1, 0, 1), self.dev(0, -1))
        self.out[-1] = self.spread(-1)
        self.out[1] = self.spread(1)
        self.share(-1, 0)
        self.share(1, 0)

    def step3(self):
        self.up2.wait_recv()
        self.down2.wait_recv()
        self.out[2] = self.spread(2)
        self.share(2, 0)

    def step4(self):
        self.far = []
        for first_off in (0, -1, 1, 2):
            up, down = self.out[first_off]
            up.wait_recv()
            self.far.append(self.put(self.block(first_off, -1, 0), self.dev(1, 1)))
            down.wait_recv()
            self.far.append(self.put(self.block(first_off, 1, 1), self.dev(1, -1)))
            self.share(first_off, -1)
            self.share(first_off, 1)

    def step5(self):
        for k, first_off in enumerate((0, -1, 1, 2)):
            self.far[2 * k].wait_recv()
            self.far[2 * k + 1].wait_recv()
            self.share(first_off, 2)

    def step6(self):
        for copy in self.shared:
            copy.wait_recv()


def normalised(values):
    centre = values - jnp.mean(values, axis=-1, keepdims=True)
    spread = jnp.mean(centre * centre, axis=-1, keepdims=True)
    scale = lax.rsqrt(spread + 1e-05)
    return centre * scale, scale


def first_blocks(lengths_ref):
    base = lax.axis_index("dp") * 4
    end = jnp.int32(0)
    first = [jnp.int32(0)] * 4
    for i in range(32):
        end = end + lengths_ref[i]
        first = [jnp.where(end <= base + b, end, first[b]) for b in range(4)]
    return [first[b] - base + 16 for b in range(4)]


def heads_across(tile):
    head = lax.broadcasted_iota(jnp.int32, tile.shape, 1) // HEAD_DIM
    return jnp.concatenate([jnp.where(head == h, tile, 0.0) for h in range(4)], axis=0)


def heads_together(tile):
    head = lax.broadcasted_iota(jnp.int32, (BLOCK, 256), 1) // HEAD_DIM
    return sum(jnp.where(head == h, tile[h * BLOCK:(h + 1) * BLOCK], 0.0) for h in range(4))


def causal(scores, b):
    query = lax.rem(lax.broadcasted_iota(jnp.int32, scores.shape, 0), BLOCK)
    key = lax.broadcasted_iota(jnp.int32, scores.shape, 1)
    return jnp.where(key <= query + b * BLOCK, scores, -1e30)


def outside(block, first):
    lane = lax.broadcasted_iota(jnp.int32, (1, SPAN), 1)
    return jnp.where(lane < (first - block) * BLOCK, -1e30, 0.0)


def parts(tile):
    return [tile[:, i * 128:(i + 1) * 128] for i in range(SPAN // 128)]


def pick_first(first, b):
    value = first[3]
    for k in range(3):
        value = jnp.where(b == k, first[k], value)
    return value


class Attention:
    def __init__(self, lengths_ref, q_ref, kv_ref, scratch):
        self.first = first_blocks(lengths_ref)
        self.q_ref, self.kv_ref = q_ref, kv_ref
        self.tall, self.top, self.total, self.acc = scratch

    @staticmethod
    def scratch():
        return [
            pltpu.VMEM((4, 512, 256), BF),
            pltpu.VMEM((4, 512, 128), F32),
            pltpu.VMEM((4, 512, 128), F32),
            pltpu.VMEM((4, 512, 256), F32),
        ]

    def start(self):
        for b in range(4):
            queries = self.q_ref[b * BLOCK:(b + 1) * BLOCK, :].astype(F32) * 0.125
            self.tall[b] = heads_across(queries).astype(BF)

    def add(self, slot, own=False):
        keys = rows(slot * GROUP, GROUP)

        def one(b):
            tile = nt(self.tall[b], self.kv_ref[keys, 0:256]) + outside(slot * 4, self.of_block(b))
            if own:
                tile = causal(tile, b)
            pieces = parts(tile)
            peak = jnp.max(functools.reduce(jnp.maximum, pieces), axis=1, keepdims=True)
            top = jnp.broadcast_to(peak, (512, 128))
            if not own:
                top = jnp.maximum(top, self.top[b])
            weights = [jnp.exp(piece - top) for piece in pieces]
            low = jnp.concatenate([piece.astype(BF) for piece in weights], axis=1)
            product = nn(low, self.kv_ref[keys, 256:512])
            if own:
                self.total[b] = sum(weights)
                self.acc[b] = product
            else:
                shrink = jnp.exp(self.top[b] - top)
                self.total[b] = self.total[b] * shrink + sum(weights)
                self.acc[b] = self.acc[b] * jnp.concatenate([shrink, shrink], axis=1) + product
            self.top[b] = top

        def two(i, carry):
            one(2 * i)
            one(2 * i + 1)
            return carry

        lax.fori_loop(0, 2, two, 0)

    def of_block(self, b):
        return pick_first(self.first, b)

    def finish(self, ctx_ref, lse_ref):
        for b in range(4):
            sums = jnp.sum(self.total[b], axis=1, keepdims=True)
            lse_ref[b] = self.top[b] + jnp.log(sums)
            ctx_ref[b * BLOCK:(b + 1) * BLOCK, :] = heads_together(self.acc[b] * (1.0 / sums)).astype(BF)


class AttentionBack:
    def __init__(self, lengths_ref, q_ref, kv_ref, ctx_ref, lse_ref, dctx_ref, scratch):
        self.first = first_blocks(lengths_ref)
        self.q_ref, self.kv_ref, self.ctx_ref = q_ref, kv_ref, ctx_ref
        self.lse_ref, self.dctx_ref = lse_ref, dctx_ref
        self.tall_q, self.tall_g, self.inner, self.acc, self.sum = scratch
        self.sum[...] = jnp.zeros_like(self.sum)

    @staticmethod
    def scratch():
        return [
            pltpu.VMEM((2048, 256), BF),
            pltpu.VMEM((2048, 256), BF),
            pltpu.VMEM((4, 512, 128), F32),
            pltpu.VMEM((4, 512, 256), F32),
            pltpu.VMEM((512, 512), F32),
        ]

    def start(self):
        for b in range(4):
            block, tall = slice(b * BLOCK, (b + 1) * BLOCK), slice(b * 512, (b + 1) * 512)
            grads = self.dctx_ref[block, :].astype(F32)
            self.tall_q[tall, :] = heads_across(self.q_ref[block, :].astype(F32) * 0.125).astype(BF)
            self.tall_g[tall, :] = heads_across(grads).astype(BF)
            product = heads_across(grads * self.ctx_ref[block, :].astype(F32))
            self.inner[b] = jnp.broadcast_to(jnp.sum(product, axis=1, keepdims=True), (512, 128))
            self.acc[b] = jnp.zeros((512, 256), F32)

    def add(self, slot, dkv, own=False):
        keys = rows(slot * GROUP, GROUP)

        def one(b):
            tall = rows(b * 512, 512)
            tile = nt(self.tall_q[tall, :], self.kv_ref[keys, 0:256])
            tile = tile + outside(slot * 4, pick_first(self.first, b))
            if own:
                tile = causal(tile, b)
            weight = jnp.exp(tile - jnp.concatenate([self.lse_ref[b]] * 4, axis=1))
            grad = nt(self.tall_g[tall, :], self.kv_ref[keys, 256:512])
            low = (weight * (grad - jnp.concatenate([self.inner[b]] * 4, axis=1))).astype(BF)
            self.acc[b] += nn(low, self.kv_ref[keys, 0:256])
            grads = tn(low, self.tall_q[tall, :]), tn(weight.astype(BF), self.tall_g[tall, :])
            for k, grad in enumerate(grads):
                cols = slice(k * 256, (k + 1) * 256)
                self.sum[:, cols] = jnp.where(b == 0, 0.0, self.sum[:, cols]) + grad

        def each(b, carry):
            one(b)
            return carry

        lax.fori_loop(0, 4, each, 0)
        dkv[keys, :] = self.sum[...].astype(BF)

    def finish(self, dq):
        for b in range(4):
            dq[b * BLOCK:(b + 1) * BLOCK, :] = heads_together(self.acc[b] * 0.125).astype(BF)


def one_hot(shape, offset):
    row = lax.broadcasted_iota(jnp.int32, shape, 0)
    lane = lax.broadcasted_iota(jnp.int32, shape, 1)
    return jnp.where(lane == row + offset, 1.0, 0.0).astype(F32)


def exact(a, b):
    return jnp.dot(a, b, precision=lax.Precision.HIGHEST, preferred_element_type=F32)


def first_kernel(
    lengths_ref, x_ref, cot_ref, wqkv_ref, wout_ref, wfc_ref, gains_ref, shifts_ref, bqv_ref, bfc_ref,
    q_ref, kv_ref, vec_ref, ctx_ref, lse_ref, n1_out, xg_out, cotg_out, wqkv_out, wo_out, wfc_out,
    n1, xg, cotg, wq, wo, wfc, vz, vall, bias, mid, out_sem, send_sem, recv_sem, *scratch,
):
    p = Place()
    mine = rows(p.dp * 32, 32)
    for j in range(3):
        wq[mine, j * 256:(j + 1) * 256] = wqkv_ref[j]
    wq[mine, 768:1024] = wout_ref[...]
    wfc[mine, :] = wfc_ref[...]
    xg[rows(p.z * BLOCK, BLOCK), :] = x_ref[...]
    cotg[rows(p.z * BLOCK, BLOCK), :] = cot_ref[...]
    place8 = one_hot((8, 128), lax.rem(p.dp * 4 + p.z, 16) * 8)
    own = vz.at[p.z]
    own[...] = jnp.zeros((8, 128), F32)
    own[0:2] = exact(gains_ref[...], place8)
    own[2:6] = exact(shifts_ref[...], place8)
    tile = vall.at[p.c, p.chip]
    tile[8:16] = jnp.zeros((8, 128), F32)
    tile[8:9] = exact(bfc_ref[...].astype(F32), one_hot((32, 128), lax.rem(p.dp, 4) * 32))
    tile[9:11] = exact(bqv_ref[...].astype(F32), one_hot((8, 128), lax.rem(p.dp, 16) * 8))
    greet(
        [p.at(dz=1), p.at(dz=-1), p.at(dz=2), p.at(dx=1), p.at(dx=-1), p.at(dx=2),
         p.at(dy=1), p.at(dy=-1), p.at(dy=2), p.at(flip=True), p.linear(1), p.linear(-1),
         p.beside(1, 2), p.beside_source()]
    )
    copies = Copies(send_sem, recv_sem)
    head = DirectGather(copies, p, wq)
    head.start()
    small = [copies.put(own, own, p.at(dz=dz)) for dz in (1, -1, 2)]
    ring = RingGather(copies, p, xg)
    ring.start()
    tail = PlaneGather(copies, p, wfc, 0, 1024)
    for copy in small:
        copy.wait_recv()
    tile[0:8] = vz[0] + vz[1] + vz[2] + vz[3]
    small = [copies.put(tile, tile, p.at(dy=dy)) for dy in (1, -1, 2)]
    head.step1()
    tail.start()
    for copy in small:
        copy.wait_recv()
    line = vall.at[p.c, rows(p.x * 4, 4)]
    small = [copies.put(line, line, p.at(dx=dx)) for dx in (1, -1, 2)]
    ring.below()
    ring.above()
    cot_ring = RingGather(copies, p, cotg)
    cot_ring.start()
    for copy in small:
        copy.wait_recv()
    plane = vall.at[p.c]
    last = copies.put(plane, plane, p.at(flip=True))
    head.step2()
    tail.step1()
    ring.far()
    last.wait_recv()
    lanes = []
    for k in range(8):
        total = vall[0, 2 * k] + vall[0, 2 * k + 1] + vall[1, 2 * k] + vall[1, 2 * k + 1]
        vec_ref[:, k * 128:(k + 1) * 128] = total
        lanes.append(total)
    for h in range(2):
        bias[:, h * 128:(h + 1) * 128] = lanes[4 * h] + lanes[4 * h + 1] + lanes[4 * h + 2] + lanes[4 * h + 3]

    def norm_block(k, carry):
        block = rows(lax.rem(p.z + k, 4) * BLOCK, BLOCK)
        hat, _ = normalised(xg[block, :].astype(F32))
        n1[block, :] = (hat * vec_ref[0:1, :] + vec_ref[2:3, :]).astype(BF)
        return carry

    lax.fori_loop(0, 4, norm_block, 0)
    cot_ring.below()
    cot_ring.above()
    head.step3()

    def start_of(k):
        return lax.rem(p.z + k, 4) * BLOCK

    sibling = p.at(flip=True)
    near, there, cross = {}, {}, []
    for pair in ((2, 0), (3, 1)):
        values = jnp.concatenate([n1[rows(start_of(k), BLOCK), :] for k in pair], axis=0)
        keys = nn(values, wq[:, 256:512]).astype(BF)
        vals = (nn(values, wq[:, 512:768]) + bias[10:11, :]).astype(BF)
        for i, k in enumerate(pair):
            ours = rows(4 * GROUP + start_of(k), BLOCK)
            kv_ref[ours, 0:256] = keys[i * BLOCK:(i + 1) * BLOCK]
            kv_ref[ours, 256:512] = vals[i * BLOCK:(i + 1) * BLOCK]
            if k < 2:
                there[k] = copies.put(kv_ref.at[ours], mid.at[k], p.at(dy=-1))
            else:
                near[k] = copies.put(
                    kv_ref.at[ours], kv_ref.at[rows(2 * GROUP + start_of(k), BLOCK)], p.linear(1)
                )
    for k in (0, 1):
        ours = kv_ref.at[rows(4 * GROUP + start_of(k), BLOCK)]
        near[k] = copies.put(ours, kv_ref.at[rows(2 * GROUP + start_of(k), BLOCK)], p.linear(1))
    wo[rows(p.z * D, D), :] = wq[:, 768:1024]
    wo_ring = RingGather(copies, p, wo, D)
    wo_ring.start()
    tail.step2()
    q_ref[...] = (nn(n1[...], wq[:, 0:256]) + bias[9:10, :]).astype(BF)
    saves = [
        pltpu.make_async_copy(source, target, out_sem.at[i])
        for i, (source, target) in enumerate(
            (
                (n1, n1_out), (xg, xg_out), (wq.at[:, 0:768], wqkv_out), (cotg, cotg_out),
                (wo, wo_out), (wfc, wfc_out),
            )
        )
    ]
    for i in range(3):
        saves[i].start()
    heads = Attention(lengths_ref, q_ref, kv_ref, scratch)
    heads.start()
    heads.add(4, own=True)
    far = {}
    for k in (0, 1):
        there[k].wait_recv()
        far[k] = copies.put(mid.at[k], kv_ref.at[rows(start_of(k), BLOCK)], p.beside(1, 2))

    def pass_near(k, onward):
        near[k].wait_recv()
        ref = kv_ref.at[rows(2 * GROUP + start_of(k), BLOCK)]
        if onward:
            far[k] = copies.put(ref, kv_ref.at[rows(start_of(k), BLOCK)], p.linear(1))
        cross.append(
            copies.put(ref, kv_ref.at[rows((1 + 2 * p.c) * GROUP + start_of(k), BLOCK)], sibling)
        )

    pass_near(2, True)
    pass_near(3, True)
    tail.step3()
    cot_ring.far()
    saves[3].start()
    tail.step4()
    pass_near(0, False)
    pass_near(1, False)
    wo_ring.below()
    wo_ring.above()

    def pass_far(k):
        far[k].wait_recv()
        cross.append(
            copies.put(
                kv_ref.at[rows((4 - 4 * p.c) * GROUP + start_of(k), BLOCK)],
                kv_ref.at[rows((3 - 2 * p.c) * GROUP + start_of(k), BLOCK)],
                sibling,
            )
        )

    heads.add(2)
    pass_far(0)
    pass_far(1)
    tail.step5()
    for copy in cross[:4]:
        copy.wait_recv()
    heads.add(3 - 2 * p.c)
    pass_far(2)
    pass_far(3)
    tail.step6()
    saves[5].start()
    heads.add(0)
    wo_ring.far()
    saves[4].start()
    for copy in cross[4:]:
        copy.wait_recv()
    heads.add(1 + 2 * p.c)
    heads.finish(ctx_ref, lse_ref)
    for save in saves:
        save.wait()
    copies.finish()


N1_COPIES = 31 + 36 + 10 + 12 + 18


def vm(count):
    return [pl.BlockSpec(memory_space=pltpu.VMEM)] * count


def far_memory(count):
    return [pl.BlockSpec(memory_space=pl.ANY)] * count


def call_first(*operands):
    shape = jax.ShapeDtypeStruct
    return pl.pallas_call(
        first_kernel,
        out_shape=(
            shape((GROUP, 256), BF),
            shape((5 * GROUP, 512), BF),
            shape((16, D), F32),
            shape((GROUP, 256), BF),
            shape((4, 512, 128), F32),
            shape((GROUP, D), BF),
            shape((GROUP, D), BF),
            shape((GROUP, D), BF),
            shape((D, 768), BF),
            shape((4 * D, 256), BF),
            shape((D, D), BF),
        ),
        in_specs=[pl.BlockSpec(memory_space=pltpu.SMEM)] + vm(9),
        out_specs=tuple(vm(5) + far_memory(6)),
        scratch_shapes=[
            pltpu.VMEM((GROUP, D), BF),
            pltpu.VMEM((GROUP, D), BF),
            pltpu.VMEM((GROUP, D), BF),
            pltpu.VMEM((D, 1024), BF),
            pltpu.VMEM((4 * D, 256), BF),
            pltpu.VMEM((D, D), BF),
            pltpu.VMEM((4, 8, 128), F32),
            pltpu.VMEM((2, 16, 16, 128), F32),
            pltpu.VMEM((16, 256), F32),
            pltpu.VMEM((2, BLOCK, 512), BF),
            pltpu.SemaphoreType.DMA((6,)),
            pltpu.SemaphoreType.DMA((N1_COPIES,)),
            pltpu.SemaphoreType.DMA((N1_COPIES,)),
            *Attention.scratch(),
        ],
        compiler_params=pltpu.CompilerParams(
            collective_id=1, has_side_effects=True, vmem_limit_bytes=VMEM_LIMIT
        ),
        name="gather_and_project",
    )(*operands)


class PlaneScatter:
    copies_needed = 18

    def __init__(self, copies, place, g, scratch):
        self.copies, self.place, self.g = copies, place, g
        self.land, self.far, self.near, self.t, self.far2, self.near2, self.last, self.rest = scratch
        self.half = g.shape[1] // 2

    @staticmethod
    def scratch(width):
        half = width // 2
        return [
            pltpu.VMEM((1024, half), BF),
            pltpu.VMEM((2, 2, 64, half), BF),
            pltpu.VMEM((2, 4, 64, half), BF),
            pltpu.VMEM((4, 64, half), BF),
            pltpu.VMEM((2, 32, half), BF),
            pltpu.VMEM((2, 64, half), BF),
            pltpu.VMEM((32, half), F32),
            pltpu.VMEM((32, half), F32),
        ]

    def dev(self, axis, step):
        c = self.place.c
        if axis == 0:
            return self.place.at(dx=(1 - c) * step, dy=c * step)
        return self.place.at(dx=c * step, dy=(1 - c) * step)

    def first(self, step):
        p = self.place
        return lax.rem(p.x * (1 - p.c) + p.y * p.c + step + 4, 4)

    def second(self, step):
        p = self.place
        return lax.rem(p.y * (1 - p.c) + p.x * p.c + step + 4, 4)

    def block(self, f, s):
        c = self.place.c
        x, y = f * (1 - c) + s * c, s * (1 - c) + f * c
        return rows((x * 4 + y) * 64, 64)

    def start(self):
        c = self.place.c
        other = pl.ds(pl.multiple_of((1 - c) * self.half, 128), self.half)
        self.swap = self.copies.put(self.g.at[:, other], self.land, self.place.at(flip=True))

    def step1(self):
        self.swap.wait_recv()
        mine = pl.ds(pl.multiple_of(self.place.c * self.half, 128), self.half)
        self.mine = mine

        def join(k, carry):
            f = self.first(2 + k // 4)
            block = self.block(f, lax.rem(k, 4))
            self.land[block, :] = (self.land[block, :].astype(F32) + self.g[block, mine].astype(F32)).astype(BF)
            return carry

        lax.fori_loop(0, 4, join, 0)
        self.out = []
        for s in range(4):
            to = self.dev(0, 1 if s < 2 else -1)
            self.out.append(
                self.copies.put(self.land.at[self.block(self.first(2), s)], self.far.at[s // 2, s % 2], to)
            )
        lax.fori_loop(4, 16, join, 0)

    def step2(self):
        self.out2 = []
        for side, step in ((0, 1), (1, -1)):
            f = self.first(step)
            for s in range(4):
                block = self.block(f, s)
                if s // 2 == side:
                    self.out[s].wait_recv()
                    self.land[block, :] = (
                        self.land[block, :].astype(F32) + self.far[side, s % 2].astype(F32)
                    ).astype(BF)
                self.out2.append(
                    self.copies.put(self.land.at[block], self.near.at[side, s], self.dev(0, step))
                )

    def step3(self):
        f = self.first(0)
        for copy in self.out2:
            copy.wait_recv()

        def total(k, carry):
            s = self.second(2 + k)
            self.t[s] = (
                self.land[self.block(f, s), :].astype(F32)
                + self.near[0, s].astype(F32)
                + self.near[1, s].astype(F32)
            ).astype(BF)
            return carry

        lax.fori_loop(0, 1, total, 0)
        s = self.second(2)
        self.up = self.copies.put(self.t.at[s, 0:32], self.far2.at[0], self.dev(1, 1))
        self.down = self.copies.put(self.t.at[s, 32:64], self.far2.at[1], self.dev(1, -1))
        lax.fori_loop(1, 4, total, 0)

    def step4(self):
        s = self.second(1)
        self.up.wait_recv()
        self.t[s, 0:32] = (self.t[s, 0:32].astype(F32) + self.far2[0].astype(F32)).astype(BF)
        self.up2 = self.copies.put(self.t.at[s], self.near2.at[0], self.dev(1, 1))
        s = self.second(-1)
        self.down.wait_recv()
        self.t[s, 32:64] = (self.t[s, 32:64].astype(F32) + self.far2[1].astype(F32)).astype(BF)
        self.down2 = self.copies.put(self.t.at[s], self.near2.at[1], self.dev(1, -1))

    def part(self, c):
        half = rows(c * 32, 32)
        return (
            self.t[self.second(0), half].astype(F32)
            + self.near2[0, half].astype(F32)
            + self.near2[1, half].astype(F32)
        )

    def step5(self):
        self.up2.wait_recv()
        self.down2.wait_recv()
        c = self.place.c
        self.last[...] = self.part(1 - c)
        self.back = self.copies.put(self.last, self.rest, self.place.at(flip=True))

    def step6(self, out):
        out[:, self.mine] = self.part(self.place.c)
        self.back.wait_recv()
        other = pl.ds(pl.multiple_of((1 - self.place.c) * self.half, 128), self.half)
        out[:, other] = self.rest[...]


class QuickScatter:
    copies_needed = 17

    def __init__(self, copies, place, g, scratch):
        self.copies, self.place, self.g = copies, place, g
        self.land, self.near, self.t, self.near2, self.last, self.rest = scratch
        self.half = g.shape[1] // 2

    @staticmethod
    def scratch(width):
        half = width // 2
        return [
            pltpu.VMEM((1024, half), BF),
            pltpu.VMEM((3, 4, 64, half), BF),
            pltpu.VMEM((4, 64, half), BF),
            pltpu.VMEM((3, 64, half), BF),
            pltpu.VMEM((32, half), F32),
            pltpu.VMEM((32, half), F32),
        ]

    dev, first, second, block, start = (
        PlaneScatter.dev, PlaneScatter.first, PlaneScatter.second, PlaneScatter.block, PlaneScatter.start
    )

    def step1(self):
        self.swap.wait_recv()
        self.mine = pl.ds(pl.multiple_of(self.place.c * self.half, 128), self.half)
        self.out = []
        for i, step in enumerate((2, 1, -1, 0)):
            f = self.first(step)

            def join(s, carry):
                block = self.block(f, s)
                self.land[block, :] = (
                    self.land[block, :].astype(F32) + self.g[block, self.mine].astype(F32)
                ).astype(BF)
                return carry

            lax.fori_loop(0, 4, join, 0)
            if step:
                for s in range(4):
                    self.out.append(
                        self.copies.put(self.land.at[self.block(f, s)], self.near.at[i, s], self.dev(0, step))
                    )

    def step2(self):
        for copy in self.out:
            copy.wait_recv()
        f = self.first(0)

        def total(s, carry):
            value = self.land[self.block(f, s), :].astype(F32)
            for i in range(3):
                value = value + self.near[i, s].astype(F32)
            self.t[s] = value.astype(BF)
            return carry

        lax.fori_loop(0, 4, total, 0)
        self.out2 = [
            self.copies.put(self.t.at[self.second(step)], self.near2.at[i], self.dev(1, step))
            for i, step in enumerate((2, 1, -1))
        ]

    def part(self, c):
        half = rows(c * 32, 32)
        value = self.t[self.second(0), half].astype(F32)
        for i in range(3):
            value = value + self.near2[i, half].astype(F32)
        return value

    def step3(self):
        for copy in self.out2:
            copy.wait_recv()
        self.last[...] = self.part(1 - self.place.c)
        self.back = self.copies.put(self.last, self.rest, self.place.at(flip=True))

    step4 = PlaneScatter.step6


class RingScatter:
    copies_needed = 4

    def __init__(self, copies, place, scratch):
        self.copies, self.place = copies, place
        self.part, self.far, self.near = scratch

    @staticmethod
    def scratch():
        return [
            pltpu.VMEM((3, BLOCK, D), BF),
            pltpu.VMEM((2, 64, D), BF),
            pltpu.VMEM((2, BLOCK, D), BF),
        ]

    def send_far(self):
        p, c = self.place, self.copies
        self.up = c.put(self.part.at[2, 0:64], self.far.at[0], p.at(dz=1))
        self.down = c.put(self.part.at[2, 64:128], self.far.at[1], p.at(dz=-1))

    def send_above(self):
        self.up.wait_recv()
        self.part[0, 0:64] = (self.part[0, 0:64].astype(F32) + self.far[0].astype(F32)).astype(BF)
        self.up2 = self.copies.put(self.part.at[0], self.near.at[0], self.place.at(dz=1))

    def send_below(self):
        self.down.wait_recv()
        self.part[1, 64:128] = (self.part[1, 64:128].astype(F32) + self.far[1].astype(F32)).astype(BF)
        self.down2 = self.copies.put(self.part.at[1], self.near.at[1], self.place.at(dz=-1))

    def received(self):
        self.up2.wait_recv()
        self.down2.wait_recv()
        return self.near[0].astype(F32) + self.near[1].astype(F32)


class RingReturn:
    copies_needed = 6

    def __init__(self, copies, place, scratch):
        self.copies, self.place = copies, place
        self.above, self.below, self.across, self.near, self.mid, self.far = scratch

    @staticmethod
    def scratch():
        return [
            pltpu.VMEM((2, BLOCK, D), BF),
            pltpu.VMEM((2, 64, D), BF),
            pltpu.VMEM((BLOCK, D), BF),
        ]

    def send_above(self):
        self.up = self.copies.put(self.above, self.near.at[0], self.place.at(dz=1))

    def send_below(self):
        self.down = self.copies.put(self.below, self.near.at[1], self.place.at(dz=-1))

    def send_far(self):
        p, c = self.place, self.copies
        self.up1 = c.put(self.across.at[0:64], self.mid.at[0], p.at(dz=1))
        self.down1 = c.put(self.across.at[64:128], self.mid.at[1], p.at(dz=-1))

    def pass_on(self):
        p, c = self.place, self.copies
        self.up1.wait_recv()
        self.up2 = c.put(self.mid.at[0], self.far.at[0:64], p.at(dz=1))
        self.down1.wait_recv()
        self.down2 = c.put(self.mid.at[1], self.far.at[64:128], p.at(dz=-1))

    def received(self):
        for copy in (self.up, self.down, self.up2, self.down2):
            copy.wait_recv()
        return self.near[0].astype(F32) + self.near[1].astype(F32) + self.far[...].astype(F32)


def norm_back(hat, scale, grad, gain):
    inner = grad * gain
    mean = jnp.mean(inner, axis=-1, keepdims=True)
    along = jnp.mean(inner * hat, axis=-1, keepdims=True)
    return (
        scale * (inner - mean - hat * along),
        jnp.sum(grad * hat, axis=0, keepdims=True),
        jnp.sum(grad, axis=0, keepdims=True),
    )


def weight_grad(left, right, out, first):
    width = right.shape[1]

    def tile(k, carry):
        turned = left[:, pl.ds(pl.multiple_of(k * 256, 256), 256)].astype(F32).T.astype(BF)
        out[rows(k * 256, 256), first:first + width] = nn(turned, right[...]).astype(BF)
        return carry

    lax.fori_loop(0, 4, tile, 0)


def middle_kernel(
    x_ref, ctx_ref, vec_ref, wproj_ref, wo_any, wfc_any, cotg_any,
    gafter_ref, gaf_ref, dctx_ref, sums_ref, res_ref, outs_ref, dw_any,
    wo, wfc, wproj, cotg, ctxf, n2g, act, dpre, dact, part, back, own, after, dw, dctx, io_sem, send_sem, recv_sem,
    *scratch,
):
    p = Place()
    loads = [
        pltpu.make_async_copy(source, target, io_sem.at[i])
        for i, (source, target) in enumerate(((wo_any, wo), (cotg_any, cotg), (wfc_any, wfc)))
    ]
    for load in loads:
        load.start()
    wproj[rows(p.dp * 32, 32), :] = wproj_ref[...]
    greet(
        [p.at(dz=1), p.at(dz=-1), p.at(dz=2), p.at(dx=1), p.at(dx=-1), p.at(dx=2),
         p.at(dy=1), p.at(dy=-1), p.at(dy=2), p.at(flip=True)]
    )
    copies = Copies(send_sem, recv_sem)
    backs = RingReturn(copies, p, (part.at[0], part.at[1], part.at[2]) + scratch)

    def block(dz):
        return rows(lax.rem(p.z + dz + 4, 4) * BLOCK, BLOCK)

    swaps = [
        copies.put(ctx_ref.at[block(dz)], ctxf.at[p.z], p.at(dz=dz)) for dz in (2, 1, -1)
    ]
    plane = DirectGather(copies, p, wproj)
    plane.start()
    ctxf[p.z] = ctx_ref[block(0), :]
    for load in loads:
        load.wait()

    plane.step1()
    for copy in swaps:
        copy.wait_recv()
    total = x_ref[...].astype(F32) + vec_ref[4:5, :]
    for k in range(4):
        total = total + nt(ctxf[k], wo[k * D:(k + 1) * D, :])
    after[...] = total
    hat, scale = normalised(after[...])
    n2g[block(0), :] = (hat * vec_ref[1:2, :] + vec_ref[3:4, :]).astype(BF)
    ring = RingGather(copies, p, n2g)
    ring.start()
    plane.step2()
    plane.step3()

    def act_grad(t, carry):
        cols = pl.ds(pl.multiple_of(t * 256, 256), 256)
        dact[:, cols] = nn(cotg[...], wproj[:, cols])
        return carry

    lax.fori_loop(0, 4, act_grad, 0)

    def mlp(pair, put_back):
        here = [block(dz) for dz in pair]

        def both(ref, cols=slice(None)):
            return jnp.concatenate([ref[h, cols] for h in here], axis=0)

        def hidden(t, carry):
            cols = pl.ds(pl.multiple_of(t * 256, 256), 256)
            pre = nn(both(n2g), wfc[:, cols]) + vec_ref[8:9, cols]
            square = pre * pre
            bend = jnp.tanh(0.7978845608028654 * pre * (1.0 + 0.044715 * square))
            slope = 0.5 * (1.0 + bend) + 0.5 * pre * (1.0 - bend * bend) * (
                0.7978845608028654 * (1.0 + 0.134145 * square)
            )
            value = (0.5 * pre * (1.0 + bend)).astype(BF)
            grad = (both(dact, cols) * slope).astype(BF)
            for i, h in enumerate(here):
                act[h, cols] = value[i * BLOCK:(i + 1) * BLOCK]
                dpre[h, cols] = grad[i * BLOCK:(i + 1) * BLOCK]
            return carry

        lax.fori_loop(0, 4, hidden, 0)

        def project(t, carry):
            cols = pl.ds(pl.multiple_of(t * 256, 256), 256)
            value = nt(both(dpre), wfc[cols, :])
            for i in range(2):
                put_back[i](cols, value[i * BLOCK:(i + 1) * BLOCK])
            return carry

        lax.fori_loop(0, 4, project, 0)

    def into(i):
        def put(cols, value):
            part[i, :, cols] = value.astype(BF)

        return put

    def keep(cols, value):
        own[:, cols] = value

    ring.below()
    ring.above()
    mlp((1, -1), (into(0), into(1)))
    backs.send_above()
    backs.send_below()
    ring.far()
    mlp((2, 0), (into(2), keep))
    backs.send_far()
    weight_grad(n2g, dpre, dw, 0)
    backs.pass_on()
    weight_grad(cotg, act, dw, 1024)
    save = pltpu.make_async_copy(dw, dw_any, io_sem.at[3])
    save.start()
    def output_part(t, carry):
        cols = pl.ds(pl.multiple_of(t * 256, 256), 256)
        outs_ref[:, cols] = nt(act[...], wproj[cols, :]).astype(BF)
        return carry

    lax.fori_loop(0, 4, output_part, 0)
    res_ref[...] = after[...] + vec_ref[5:6, :]
    grad = own[...] + backs.received()
    hat, scale = normalised(after[...])
    grad_in, gain, shift = norm_back(hat, scale, grad, vec_ref[1:2, :])
    residual = cotg[block(0), :].astype(F32)
    back[...] = grad_in + residual
    gaf_ref[...] = back[...].astype(BF)
    for k in (2, 1, 3, 0):
        owner = lax.rem(p.z + k, 4)
        part = nn(gaf_ref[...], wo[rows(owner * D, D), :]).astype(BF)
        if k:
            dctx[k] = part
            swaps.append(copies.put(dctx.at[k], dctx_ref.at[block(0)], p.at(dz=k)))
        else:
            dctx_ref[block(0), :] = part
    sums_ref[...] = jnp.zeros_like(sums_ref)
    sums_ref[0:1, :] = gain
    sums_ref[1:2, :] = shift
    sums_ref[2:3, :] = jnp.sum(back[...], axis=0, keepdims=True)
    sums_ref[3:4, :] = jnp.sum(residual, axis=0, keepdims=True)
    sums_ref[4:5, :] = jnp.sum(dpre[...].astype(F32), axis=0, keepdims=True)
    gafter_ref[...] = back[...]

    for copy in swaps[3:]:
        copy.wait_recv()
    save.wait()
    copies.finish()


N3_COPIES = 6 + 4 + 6 + 31


def call_middle(*operands):
    shape = jax.ShapeDtypeStruct
    return pl.pallas_call(
        middle_kernel,
        out_shape=(
            shape((BLOCK, D), F32),
            shape((BLOCK, D), BF),
            shape((GROUP, 256), BF),
            shape((8, D), F32),
            shape((BLOCK, D), F32),
            shape((GROUP, D), BF),
            shape((D, 2048), BF),
        ),
        in_specs=vm(4) + far_memory(3),
        out_specs=tuple(vm(6) + far_memory(1)),
        scratch_shapes=[
            pltpu.VMEM((4 * D, 256), BF),
            pltpu.VMEM((D, D), BF),
            pltpu.VMEM((D, D), BF),
            pltpu.VMEM((GROUP, D), BF),
            pltpu.VMEM((4, BLOCK, 256), BF),
            pltpu.VMEM((GROUP, D), BF),
            pltpu.VMEM((GROUP, D), BF),
            pltpu.VMEM((GROUP, D), BF),
            pltpu.VMEM((GROUP, D), F32),
            pltpu.VMEM((3, BLOCK, D), BF),
            pltpu.VMEM((BLOCK, D), F32),
            pltpu.VMEM((BLOCK, D), F32),
            pltpu.VMEM((BLOCK, D), F32),
            pltpu.VMEM((D, 2048), BF),
            pltpu.VMEM((4, BLOCK, 256), BF),
            pltpu.SemaphoreType.DMA((4,)),
            pltpu.SemaphoreType.DMA((N3_COPIES,)),
            pltpu.SemaphoreType.DMA((N3_COPIES,)),
            *RingReturn.scratch(),
        ],
        compiler_params=pltpu.CompilerParams(
            collective_id=2, has_side_effects=True, vmem_limit_bytes=VMEM_LIMIT
        ),
        name="mlp_both_ways",
    )(*operands)


def last_kernel(
    lengths_ref, q_ref, kv_ref, lse_ref, dctx_ref, x_ref, vec_ref, gafter_ref, gaf_ref, ctx_ref, sums_ref, res_ref, outs_ref,
    n1_any, xg_any, wqkv_any, dw_any,
    gin_ref, out_ref, early_ref, mid_ref, late_ref, sums_out,
    dq, dkv, n1, xg, wqkv, gafg, cross, hand, land, mid, fin, dqkv, early, middle, late, own, hats, small_ref, xsum, ysum, zsum, line,
    io_sem, send_sem, recv_sem, *scratch,
):
    p = Place()
    loads = [
        pltpu.make_async_copy(source, target, io_sem.at[i])
        for i, (source, target) in enumerate(
            ((dw_any, early), (n1_any, n1), (wqkv_any, wqkv), (xg_any, xg))
        )
    ]
    for load in loads:
        load.start()
    gafg[rows(p.z * BLOCK, BLOCK), :] = gaf_ref[...]
    greet(
        [p.at(dz=1), p.at(dz=-1), p.at(dz=2), p.at(dx=1), p.at(dx=-1), p.at(dx=2),
         p.at(dy=1), p.at(dy=-1), p.at(dy=2), p.at(flip=True), p.linear(1), p.linear(-1),
         p.at(dy=1, flip=True), p.at(dy=-1, flip=True), p.at(dy=2, flip=True),
         p.beside(-1, -2), p.beside_source(-2, 1)]
    )
    copies = Copies(send_sem, recv_sem)
    scatter = RingScatter(copies, p, scratch[0:3])
    plane = PlaneScatter(copies, p, early, scratch[6:14])
    quick = QuickScatter(copies, p, late, scratch[14:20])
    quick2 = QuickScatter(copies, p, middle, scratch[25:31])
    sibling = p.at(flip=True)
    even = p.c == 0

    def start_of(k):
        return lax.rem(p.z + k, 4) * BLOCK

    def block(k):
        return rows(start_of(k), BLOCK)

    outs = RingReturn(
        copies, p, (outs_ref.at[block(1)], outs_ref.at[block(3)], outs_ref.at[block(2)]) + scratch[3:6]
    )

    def spread_bias(row, value):
        for half in range(2):
            for k in range(4):
                first = (4 * half + k) * 128
                small_ref[row:row + 1, first:first + 128] = value[:, half * 128:(half + 1) * 128]

    order = (2, 1, 3, 0)
    ring = RingGather(copies, p, gafg)
    ring.start()
    outs.send_above()
    outs.send_below()
    outs.send_far()
    for load in loads:
        load.wait()
    plane.start()
    heads = AttentionBack(lengths_ref, q_ref, kv_ref, ctx_ref, lse_ref, dctx_ref, scratch[20:25])
    heads.start()

    def cross_over(side):
        ref = dkv.at[rows((1 + 2 * side) * GROUP, GROUP)]
        return copies.put(ref, cross.at[side], sibling)

    heads.add(1, dkv)
    low = cross_over(0)
    heads.add(0, dkv)
    low.wait_recv()
    far, near = {}, {}
    for k in (3, 2, 0, 1):
        i = order.index(k)
        hand[0, block(k)] = (
            dkv[rows(start_of(k), BLOCK), :].astype(F32) + jnp.where(even, 0.0, cross[0, block(k)].astype(F32))
        ).astype(BF)
        if i < 2:
            far[k] = copies.put(hand.at[0, block(k)], mid.at[i], p.at(dy=1))
        else:
            far[k] = copies.put(hand.at[0, block(k)], land.at[0, block(k)], p.linear(-1))
    heads.add(3, dkv)
    high = cross_over(1)
    for i, k in enumerate(order[:2]):
        far[k].wait_recv()
        far[k] = copies.put(mid.at[i], fin.at[i], p.beside(-1, -2))
    ring.below()
    ring.above()
    outs.pass_on()
    plane.step1()
    heads.add(2, dkv)
    high.wait_recv()

    def near_sum(k):
        beside = jnp.where(even, cross[0, block(k)].astype(F32), cross[1, block(k)].astype(F32))
        return dkv[rows(2 * GROUP + start_of(k), BLOCK), :].astype(F32) + beside

    for k in order[:2]:
        hand[1, block(k)] = near_sum(k).astype(BF)
        near[k] = copies.put(hand.at[1, block(k)], land.at[1, block(k)], p.linear(-1))
    for k in order[2:]:
        far[k].wait_recv()
        hand[1, block(k)] = (near_sum(k) + land[0, block(k)].astype(F32)).astype(BF)
        near[k] = copies.put(hand.at[1, block(k)], land.at[1, block(k)], p.linear(-1))
    plane.step2()
    heads.add(4, dkv, own=True)
    heads.finish(dq)
    ring.far()
    weight_grad(n1, dq, middle, 0)
    weight_grad(gafg, ctx_ref, middle, 256)
    quick2.start()
    dqkv[:, 0:256] = dq[...]
    small_ref[...] = jnp.zeros_like(small_ref)
    small_ref[8:9, :] = sums_ref[4:5, :]
    spread_bias(9, jnp.sum(dq[...].astype(F32), axis=0, keepdims=True))
    small_ref[1:2, :] = sums_ref[0:1, :]
    small_ref[3:6, :] = sums_ref[1:4, :]
    out_ref[...] = res_ref[...] + outs_ref[block(0), :].astype(F32) + outs.received()

    def keep_hat(k, carry):
        here = rows(k * BLOCK, BLOCK)
        hats[here, :], _ = normalised(xg[here, :].astype(F32))
        return carry

    lax.fori_loop(0, 4, keep_hat, 0)
    quick2.step1()

    def own_keys(k):
        near[k].wait_recv()
        value = dkv[rows(4 * GROUP + start_of(k), BLOCK), :].astype(F32) + land[1, block(k)].astype(F32)
        value = value + jnp.where(even, cross[1, block(k)].astype(F32), 0.0)
        if k in order[:2]:
            far[k].wait_recv()
            value = value + fin[order.index(k)].astype(F32)
        dqkv[block(k), 256:768] = value.astype(BF)

    def grad_parts(first, second):
        grad = nt(jnp.concatenate([dqkv[block(first), :], dqkv[block(second), :]], axis=0), wqkv[...])
        return grad[0:BLOCK], grad[BLOCK:2 * BLOCK]

    def tally(k, grad):
        small_ref[0:1, :] += jnp.sum(grad * hats[block(k), :], axis=0, keepdims=True)
        small_ref[2:3, :] += jnp.sum(grad, axis=0, keepdims=True)

    own_keys(2)
    own_keys(1)
    across, above = grad_parts(2, 1)
    scatter.part[2] = across.astype(BF)
    scatter.send_far()
    scatter.part[0] = above.astype(BF)
    tally(2, across)
    tally(1, above)
    own_keys(3)
    own_keys(0)
    weight_grad(n1, dqkv.at[:, 256:768], late, 0)
    quick.start()
    below, here = grad_parts(3, 0)
    scatter.part[1] = below.astype(BF)
    own[...] = here
    tally(3, below)
    tally(0, here)
    spread_bias(10, jnp.sum(dqkv[:, 512:768].astype(F32), axis=0, keepdims=True))

    def lanes(x, width):
        return pl.ds(pl.multiple_of(x * width, 128), width)

    sends = []
    for i, dx in enumerate((1, -1, 2)):
        to = lax.rem(p.x + dx + 4, 4)
        sends.append(copies.put(small_ref.at[:, lanes(to, 256)], xsum.at[i], p.at(dx=dx)))
    scatter.send_above()
    scatter.send_below()
    quick2.step2()
    quick.step1()
    for copy in sends:
        copy.wait_recv()
    line[...] = small_ref[:, lanes(p.x, 256)] + xsum[0] + xsum[1] + xsum[2]
    sends = []
    for dy in (0, 1, -1, 2):
        for flip in (False, True):
            if dy or flip:
                to = lax.rem(p.y + dy + 4, 4) // 2
                sends.append(
                    copies.put(line.at[:, lanes(to, 128)], ysum.at[len(sends)], p.at(dy=dy, flip=flip))
                )
    plane.step3()
    quick.step2()
    hat, scale = normalised(x_ref[...].astype(F32))
    back, _, _ = norm_back(hat, scale, own[...] + scatter.received(), vec_ref[0:1, :])
    gin_ref[...] = gafter_ref[...] + back
    for copy in sends:
        copy.wait_recv()
    total = line[:, lanes(p.y // 2, 128)]
    for i in range(7):
        total = total + ysum[i]
    zsum[3] = total
    sends = [copies.put(zsum.at[3, 0:8], zsum.at[i, 0:8], p.at(dz=dz)) for i, dz in enumerate((1, -1, 2))]
    plane.step4()
    quick2.step3()
    quick.step3()
    plane.step5()
    for copy in sends:
        copy.wait_recv()
    sums_out[0:8] = zsum[3, 0:8] + zsum[0, 0:8] + zsum[1, 0:8] + zsum[2, 0:8]
    sums_out[8:16] = zsum[3, 8:16]
    quick2.step4(mid_ref)
    quick.step4(late_ref)
    plane.step6(early_ref)
    copies.finish()


N5_COPIES = 2 + 4 + 6 + 4 + 4 + 2 + 4 + 18 + 2 * 17 + 3 + 7 + 3


def call_last(*operands):
    shape = jax.ShapeDtypeStruct
    return pl.pallas_call(
        last_kernel,
        out_shape=(
            shape((BLOCK, D), F32),
            shape((BLOCK, D), F32),
            shape((32, 2048), F32),
            shape((32, 512), F32),
            shape((32, 512), F32),
            shape((16, 128), F32),
        ),
        in_specs=[pl.BlockSpec(memory_space=pltpu.SMEM)] + vm(12) + far_memory(4),
        out_specs=tuple(vm(6)),
        scratch_shapes=[
            pltpu.VMEM((GROUP, 256), BF),
            pltpu.VMEM((5 * GROUP, 512), BF),
            pltpu.VMEM((GROUP, D), BF),
            pltpu.VMEM((GROUP, D), BF),
            pltpu.VMEM((D, 768), BF),
            pltpu.VMEM((GROUP, D), BF),
            pltpu.VMEM((2, GROUP, 512), BF),
            pltpu.VMEM((2, GROUP, 512), BF),
            pltpu.VMEM((2, GROUP, 512), BF),
            pltpu.VMEM((2, BLOCK, 512), BF),
            pltpu.VMEM((2, BLOCK, 512), BF),
            pltpu.VMEM((GROUP, 768), BF),
            pltpu.VMEM((D, 2048), BF),
            pltpu.VMEM((D, 512), BF),
            pltpu.VMEM((D, 512), BF),
            pltpu.VMEM((BLOCK, D), F32),
            pltpu.VMEM((GROUP, D), F32),
            pltpu.VMEM((16, D), F32),
            pltpu.VMEM((3, 16, 256), F32),
            pltpu.VMEM((7, 16, 128), F32),
            pltpu.VMEM((4, 16, 128), F32),
            pltpu.VMEM((16, 256), F32),
            pltpu.SemaphoreType.DMA((4,)),
            pltpu.SemaphoreType.DMA((N5_COPIES,)),
            pltpu.SemaphoreType.DMA((N5_COPIES,)),
            *RingScatter.scratch(),
            *RingReturn.scratch(),
            *PlaneScatter.scratch(2048),
            *QuickScatter.scratch(512),
            *AttentionBack.scratch(),
            *QuickScatter.scratch(512),
        ],
        compiler_params=pltpu.CompilerParams(
            collective_id=3, has_side_effects=True, vmem_limit_bytes=VMEM_LIMIT
        ),
        name="project_back",
    )(*operands)


def finish_kernel(
    out_ref, gin_ref, early_ref, mid_ref, late_ref, small_ref,
    out, gin, wqkv, wout, wfc, wproj, bqv, bfc, gains, shifts,
):
    dp, z = lax.axis_index("dp"), lax.axis_index("tensor")
    out[...] = out_ref[...]
    gin[...] = gin_ref[...]
    wqkv[0] = mid_ref[:, 0:256]
    wqkv[1] = late_ref[:, 0:256]
    wqkv[2] = late_ref[:, 256:512]
    wout[...] = mid_ref[:, 256:512]
    wfc[...] = early_ref[:, 0:1024]
    wproj[...] = early_ref[:, 1024:2048]

    def pick(first, offset, width):
        row = lax.broadcasted_iota(jnp.int32, (128, 128), 0)
        lane = lax.broadcasted_iota(jnp.int32, (128, 128), 1)
        chosen = jnp.where(row == lane + lax.rem(offset, 128), 1.0, 0.0).astype(F32)
        return exact(small_ref[first:first + 8, :], chosen)[:, 0:width]

    eight = pick(0, (dp * 4 + z) * 8, 8)
    gains[...] = eight[0:2]
    shifts[...] = eight[2:6]
    bqv[...] = pick(8, dp * 8, 8)[1:3]
    bfc[...] = pick(8, dp * 32, 32)[0:1]


def call_finish(*operands):
    shape = jax.ShapeDtypeStruct
    return pl.pallas_call(
        finish_kernel,
        out_shape=(
            shape((BLOCK, D), F32),
            shape((BLOCK, D), F32),
            shape((3, 32, 256), F32),
            shape((32, 256), F32),
            shape((32, 1024), F32),
            shape((32, 1024), F32),
            shape((2, 8), F32),
            shape((1, 32), F32),
            shape((2, 8), F32),
            shape((4, 8), F32),
        ),
        in_specs=vm(6),
        out_specs=tuple(vm(10)),
        compiler_params=pltpu.CompilerParams(vmem_limit_bytes=VMEM_LIMIT),
        name="lay_out",
    )(*operands)


def on_device(inputs, lengths, w_qkv, w_out, w_fc, w_proj, b_qv, b_fc, gains, shifts, cotangent):
    q, kv, vec, ctx, lse, n1, xg, cotg, wqkv, wo, wfc = call_first(
        lengths, inputs, cotangent, w_qkv[0].transpose(1, 0, 2), w_out[0].T, w_fc[0],
        gains[0], shifts[0], b_qv[0], b_fc,
    )
    gafter, gaf, dctx, sums, res, outs, dw_mlp = call_middle(
        inputs, ctx, vec, w_proj[0].T, wo, wfc, cotg
    )
    gin, out, early, mid, late, small = call_last(
        lengths, q, kv, lse, dctx, inputs, vec, gafter, gaf, ctx, sums, res, outs, n1, xg, wqkv, dw_mlp
    )
    out, gin, g_qkv, g_out, g_fc, g_proj, g_bqv, g_bfc, g_gains, g_shifts = call_finish(
        out, gin, early, mid, late, small
    )
    return (
        out, gin, g_qkv.transpose(1, 0, 2)[None], g_out.T[None], g_fc[None], g_proj.T[None],
        g_bqv[None], g_bfc, g_gains[None], g_shifts[None],
    )


def solution(mesh):
    return jax.shard_map(
        on_device,
        mesh=mesh,
        in_specs=(
            P(("dp", "tensor"), None),
            P(),
            P(None, "dp", None, "tensor"),
            P(None, "tensor", "dp"),
            P(None, "dp", "tensor"),
            P(None, "tensor", "dp"),
            P(None, None, ("tensor", "dp")),
            P(None, ("tensor", "dp")),
            P(None, None, ("dp", "tensor")),
            P(None, None, ("dp", "tensor")),
            P(("dp", "tensor"), None),
        ),
        out_specs=(
            P(("dp", "tensor"), None),
            P(("dp", "tensor"), None),
            P(None, "dp", None, "tensor"),
            P(None, "tensor", "dp"),
            P(None, "dp", "tensor"),
            P(None, "tensor", "dp"),
            P(None, None, ("tensor", "dp")),
            P(None, ("tensor", "dp")),
            P(None, None, ("dp", "tensor")),
            P(None, None, ("dp", "tensor")),
        ),
        check_vma=False,
    )
```

profile of v0, /device:TPU:0, one launch (start us, length us, event | category | flops | bytes accessed | tf_op | source)
XLA Modules:
  0.0 182.6 jit_solution(230521242875352953)
XLA Ops:
  0.6 58.2 %gather_and_project.1 = (bf16[512,256]{1,0:T(8,128)(2,1)}, bf16[2560,512]{1,0:T(8,128)(2,1)}, f32[16,1024]{1,0:T(8,128)}, bf16[512,256]{1,0:T(8,128)(2,1)}, f32[...) custom-call(s32[32]{0:T(128)} %lengths_ref.3, ...), custom_call_target="tpu_custom_call" | custom-call | tf_op jit(solution)/shard_map/gather_and_project/pallas_call | solution.py:627
  58.8 51.6 %mlp_both_ways.1 = (f32[128,1024]{1,0:T(8,128)}, bf16[128,1024]{1,0:T(8,128)(2,1)}, bf16[512,256]{1,0:T(8,128)(2,1)}, f32[8,1024]{1,0:T(8,128)}, f32[128,1024]{1...) custom-call(bf16[128,1024]{1,0:T(8,128)(2,1)} %x_ref.5, bf16[512,256]{1,0:T(8,128)(2,1)} %get-tuple-element.47.ctx_ref, ...), custom_call_target="tpu_custom_call" | custom-call | tf_op jit(solution)/shard_map/mlp_both_ways/pallas_call | solution.py:1124
  110.5 69.4 %project_back.1 = (f32[128,1024]{1,0:T(8,128)}, f32[128,1024]{1,0:T(8,128)}, f32[32,2048]{1,0:T(8,128)}, f32[32,512]{1,0:T(8,128)}, f32[32,512]{1,0:T(8,128)}, /*index=5*/f32[16,128]{1,0:T(8,128)}) custom-call(s32[32]{0:T(128)} %lengths_ref.3, bf16[512,256]{1,0:T(8,128)(2,1)} %get-tuple-element.44.q_ref, bf16[2560,512]{1,0:T(8,128)(2,1)} %get-tuple-element.45.kv_ref, ...), custom_call_target="tpu_custom_call" | custom-call | tf_op jit(solution)/shard_map/project_back/pallas_call | solution.py:1377
  179.9 2.6 %lay_out.1 = (f32[128,1024]{1,0:T(8,128)}, f32[128,1024]{1,0:T(8,128)}, f32[3,32,256]{2,1,0:T(8,128)}, f32[32,256]{1,0:T(8,128)}, f32[32,1024]{1,0:T(8,128)}, /*...) custom-call(f32[128,1024]{1,0:T(8,128)} %get-tuple-element.62.out_ref, ...), custom_call_target="tpu_custom_call" | custom-call | tf_op jit(solution)/shard_map/lay_out/pallas_call | solution.py:1458
where the time goes:
time: 185 us; the launch traced here: 183 us
  Pallas kernels  182 us (98%)
    pallas_call x1, Pallas kernels, call_last(): pl.pallas_call(last_kernel, out_shape=(shape((BLOCK, D), F32), shape((BLO...  69.4 us
    pallas_call x1, Pallas kernels, call_first(): pl.pallas_call(first_kernel, out_shape=(shape((GROUP, 256), BF), shape((5...  58.2 us
    pallas_call x1, Pallas kernels, call_middle(): pl.pallas_call(middle_kernel, out_shape=(shape((BLOCK, D), F32), shape((B...  51.6 us

commit v1 on v0

--- a/solution.py
+++ b/solution.py
@@ -410,17 +410,23 @@
             grad = nt(self.tall_g[tall, :], self.kv_ref[keys, 256:512])
             low = (weight * (grad - jnp.concatenate([self.inner[b]] * 4, axis=1))).astype(BF)
             self.acc[b] += nn(low, self.kv_ref[keys, 0:256])
-            grads = tn(low, self.tall_q[tall, :]), tn(weight.astype(BF), self.tall_g[tall, :])
+            return low, weight.astype(BF)
+
+        def two(i, carry):
+            low, weights = zip(one(2 * i), one(2 * i + 1))
+            tall = rows(i * 1024, 1024)
+            grads = (
+                tn(jnp.concatenate(low, axis=0), self.tall_q[tall, :]),
+                tn(jnp.concatenate(weights, axis=0), self.tall_g[tall, :]),
+            )
             for k, grad in enumerate(grads):
                 cols = slice(k * 256, (k + 1) * 256)
-                self.sum[:, cols] = jnp.where(b == 0, 0.0, self.sum[:, cols]) + grad
-
-        def each(b, carry):
-            one(b)
+                total = jnp.where(i == 0, 0.0, self.sum[:, cols]) + grad
+                self.sum[:, cols] = total
+                dkv[keys, cols] = total.astype(BF)
             return carry
 
-        lax.fori_loop(0, 4, each, 0)
-        dkv[keys, :] = self.sum[...].astype(BF)
+        lax.fori_loop(0, 2, two, 0)
 
     def finish(self, dq):
         for b in range(4):
@@ -1018,6 +1024,8 @@
     ring = RingGather(copies, p, n2g)
     ring.start()
     plane.step2()
+    ring.below()
+    ring.above()
     plane.step3()
 
     def act_grad(t, carry):
@@ -1068,8 +1076,6 @@
     def keep(cols, value):
         own[:, cols] = value
 
-    ring.below()
-    ring.above()
     mlp((1, -1), (into(0), into(1)))
     backs.send_above()
     backs.send_below()
@@ -1215,9 +1221,6 @@
     outs.send_above()
     outs.send_below()
     outs.send_far()
-    for load in loads:
-        load.wait()
-    plane.start()
     heads = AttentionBack(lengths_ref, q_ref, kv_ref, ctx_ref, lse_ref, dctx_ref, scratch[20:25])
     heads.start()
 
@@ -1241,15 +1244,17 @@
             far[k] = copies.put(hand.at[0, block(k)], land.at[0, block(k)], p.linear(-1))
     heads.add(3, dkv)
     high = cross_over(1)
+    for load in loads:
+        load.wait()
     for i, k in enumerate(order[:2]):
         far[k].wait_recv()
         far[k] = copies.put(mid.at[i], fin.at[i], p.beside(-1, -2))
     ring.below()
     ring.above()
     outs.pass_on()
-    plane.step1()
     heads.add(2, dkv)
     high.wait_recv()
+    plane.start()
 
     def near_sum(k):
         beside = jnp.where(even, cross[0, block(k)].astype(F32), cross[1, block(k)].astype(F32))
@@ -1262,9 +1267,9 @@
         far[k].wait_recv()
         hand[1, block(k)] = (near_sum(k) + land[0, block(k)].astype(F32)).astype(BF)
         near[k] = copies.put(hand.at[1, block(k)], land.at[1, block(k)], p.linear(-1))
-    plane.step2()
     heads.add(4, dkv, own=True)
     heads.finish(dq)
+    plane.step1()
     ring.far()
     weight_grad(n1, dq, middle, 0)
     weight_grad(gafg, ctx_ref, middle, 256)
@@ -1284,6 +1289,7 @@
 
     lax.fori_loop(0, 4, keep_hat, 0)
     quick2.step1()
+    plane.step2()
 
     def own_keys(k):
         near[k].wait_recv()

time: 185 us -> 182 us (0.984)
  Pallas kernels: 182 us -> 179 us
    pallas_call x1, Pallas kernels: 69.4 us -> 66.4 us  [call_last(): pl.pallas_call(last_kernel, out_shape=(shape((BLOCK, D), F32), shape((BLO...]
where the time goes in v1:
time: 182 us; the launch traced here: 180 us
  Pallas kernels  179 us (98%)
    pallas_call x1, Pallas kernels, call_last(): pl.pallas_call(last_kernel, out_shape=(shape((BLOCK, D), F32), shape((BLO...  66.4 us
    pallas_call x1, Pallas kernels, call_first(): pl.pallas_call(first_kernel, out_shape=(shape((GROUP, 256), BF), shape((5...  58.2 us
    pallas_call x1, Pallas kernels, call_middle(): pl.pallas_call(middle_kernel, out_shape=(shape((BLOCK, D), F32), shape((B...  51.8 us

profile of v1, /device:TPU:0, one launch (start us, length us, event | category | flops | bytes accessed | tf_op | source)
XLA Modules:
  0.0 179.7 jit_solution(7667553237856881920)
XLA Ops:
  0.6 58.2 %gather_and_project.1 = (bf16[512,256]{1,0:T(8,128)(2,1)}, bf16[2560,512]{1,0:T(8,128)(2,1)}, f32[16,1024]{1,0:T(8,128)}, bf16[512,256]{1,0:T(8,128)(2,1)}, f32[...) custom-call(s32[32]{0:T(128)} %lengths_ref.3, ...), custom_call_target="tpu_custom_call" | custom-call | tf_op jit(solution)/shard_map/gather_and_project/pallas_call | solution.py:633
  58.8 51.8 %mlp_both_ways.1 = (f32[128,1024]{1,0:T(8,128)}, bf16[128,1024]{1,0:T(8,128)(2,1)}, bf16[512,256]{1,0:T(8,128)(2,1)}, f32[8,1024]{1,0:T(8,128)}, f32[128,1024]{1...) custom-call(bf16[128,1024]{1,0:T(8,128)(2,1)} %x_ref.5, bf16[512,256]{1,0:T(8,128)(2,1)} %get-tuple-element.47.ctx_ref, ...), custom_call_target="tpu_custom_call" | custom-call | tf_op jit(solution)/shard_map/mlp_both_ways/pallas_call | solution.py:1130
  110.6 66.4 %project_back.1 = (f32[128,1024]{1,0:T(8,128)}, f32[128,1024]{1,0:T(8,128)}, f32[32,2048]{1,0:T(8,128)}, f32[32,512]{1,0:T(8,128)}, f32[32,512]{1,0:T(8,128)}, /*index=5*/f32[16,128]{1,0:T(8,128)}) custom-call(s32[32]{0:T(128)} %lengths_ref.3, bf16[512,256]{1,0:T(8,128)(2,1)} %get-tuple-element.44.q_ref, bf16[2560,512]{1,0:T(8,128)(2,1)} %get-tuple-element.45.kv_ref, ...), custom_call_target="tpu_custom_call" | custom-call | tf_op jit(solution)/shard_map/project_back/pallas_call | solution.py:1383
  177.0 2.6 %lay_out.1 = (f32[128,1024]{1,0:T(8,128)}, f32[128,1024]{1,0:T(8,128)}, f32[3,32,256]{2,1,0:T(8,128)}, f32[32,256]{1,0:T(8,128)}, f32[32,1024]{1,0:T(8,128)}, /*...) custom-call(f32[128,1024]{1,0:T(8,128)} %get-tuple-element.62.out_ref, ...), custom_call_target="tpu_custom_call" | custom-call | tf_op jit(solution)/shard_map/lay_out/pallas_call | solution.py:1464
